TPU v7x, 1024 devices: a whole 4x4x32 slice. The times are simulated.
1024 devices in a mesh: group: 32 (over y, x, core), ep: 32 (over z).
Axes of the slice: x: 4, y: 4, z: 32, core: 2. Of those that a mesh axis runs over, the one named last changes fastest.
Arguments:
- tokens: bfloat16 [131072, 2048], P(('group', 'ep')), may hold values from -6 to 6
- cotangent: bfloat16 [131072, 2048], P(('group', 'ep')), may hold values from -12 to 12
- gate_prob: bfloat16 [131072, 1], P(('group', 'ep')), may hold values from 0.099609375 to 1
- expert_ids: int32 [131072, 1], P(('group', 'ep')), may hold values from 0 to 31; in each aligned block of 128 rows (0 to 127, 128 to 255, ...) at most 5 rows name the same one
- gate_weight: bfloat16 [32, 2048, 512], P('ep'), may hold values from -0.125 to 0.125
- up_weight: bfloat16 [32, 2048, 512], P('ep'), may hold values from -0.125 to 0.125
- down_weight: bfloat16 [32, 2048, 512], P('ep'), may hold values from -0.25 to 0.25
Outputs:
- grad_tokens: bfloat16 [131072, 2048], P(('group', 'ep'))
- grad_prob: bfloat16 [131072, 1], P(('group', 'ep'))
- grad_gate: float32 [32, 2048, 512], P('ep', 'group')
- grad_up: float32 [32, 2048, 512], P('ep', 'group')
- grad_down: float32 [32, 2048, 512], P('ep', 'group')
Inputs may be any that keep to these rules, and one draw needn't show every extreme that they name: `expert_ids`: among the 128 rows of one device no expert is named more than 5 times, a bound that some block reaches; every expert is named by some row.
All inputs are finite; a program needn't handle non-finite values.
Results may differ from a plain program's by a relative error of at most 0.018.
Values may be sent and summed in bfloat16 or wider, within the bound.
A program may use at most 64 MiB of HBM per device.

v0:
```python
import jax
import jax.numpy as jnp
from jax import lax
from jax.sharding import PartitionSpec as P


def slot_index(expert_col, ep_count, capacity):
    hits = (expert_col[:, None] == jnp.arange(ep_count, dtype=jnp.int32)[None, :]).astype(jnp.int32)
    before = jnp.cumsum(hits, axis=0) - hits
    return expert_col * capacity + jnp.sum(before * hits, axis=1)


def expert_work(x_rows, dy_rows, p_rows, weights):
    w_gate = weights[0][0]
    w_up = weights[1][0]
    w_down = weights[2][0]
    width = x_rows.shape[-1]
    leading = x_rows.shape[:2]
    flat_x = x_rows.reshape(-1, width)
    flat_dy = dy_rows.reshape(-1, width)
    flat_p = p_rows.reshape(-1)
    contract_h = (((1,), (1,)), ((), ()))
    gate_pre = jnp.dot(flat_x, w_gate, preferred_element_type=jnp.float32)
    up_pre = jnp.dot(flat_x, w_up, preferred_element_type=jnp.float32)
    sig_gate = jax.nn.sigmoid(gate_pre)
    active = gate_pre * sig_gate
    hidden = (active * up_pre).astype(jnp.bfloat16)
    restored = lax.dot_general(hidden, w_down, contract_h, preferred_element_type=jnp.float32)
    dy_float = flat_dy.astype(jnp.float32)
    back_prob = jnp.sum(dy_float * restored, axis=1).astype(jnp.bfloat16)
    scaled = (flat_p.astype(jnp.float32)[:, None] * dy_float).astype(jnp.bfloat16)
    back_hidden = jnp.dot(scaled, w_down, preferred_element_type=jnp.float32)
    back_gate = (back_hidden * up_pre * sig_gate * (1.0 + gate_pre * (1.0 - sig_gate))).astype(
        jnp.bfloat16
    )
    back_up = (back_hidden * active).astype(jnp.bfloat16)
    back_rows = (
        lax.dot_general(back_gate, w_gate, contract_h, preferred_element_type=jnp.float32)
        + lax.dot_general(back_up, w_up, contract_h, preferred_element_type=jnp.float32)
    ).astype(jnp.bfloat16)
    return (
        back_rows.reshape(leading + (width,)),
        back_prob.reshape(leading),
        back_gate.reshape(leading + (-1,)),
        back_up.reshape(leading + (-1,)),
        hidden.reshape(leading + (-1,)),
        scaled.reshape(leading + (width,)),
        x_rows,
    )


def per_device(tokens, cotangent, gate_prob, expert_ids, gate_weight, up_weight, down_weight):
    ep_count = lax.axis_size("ep")
    tok_count, width = tokens.shape
    capacity = tok_count // ep_count + max(1, tok_count // (4 * ep_count))
    slots_all = ep_count * capacity
    target = slot_index(expert_ids[:, 0], ep_count, capacity)
    send_x = (
        jnp.zeros((slots_all, width), jnp.bfloat16)
        .at[target]
        .set(tokens)
        .reshape(ep_count, capacity, width)
    )
    send_dy = (
        jnp.zeros((slots_all, width), jnp.bfloat16)
        .at[target]
        .set(cotangent)
        .reshape(ep_count, capacity, width)
    )
    send_p = (
        jnp.zeros((slots_all,), jnp.bfloat16)
        .at[target]
        .set(gate_prob[:, 0])
        .reshape(ep_count, capacity)
    )
    weights = (gate_weight, up_weight, down_weight)
    arrived = (
        lax.all_to_all(send_x, "ep", split_axis=0, concat_axis=0, tiled=True),
        lax.all_to_all(send_dy, "ep", split_axis=0, concat_axis=0, tiled=True),
        lax.all_to_all(send_p, "ep", split_axis=0, concat_axis=0, tiled=True),
    )
    produced = expert_work(arrived[0], arrived[1], arrived[2], weights)
    returned_rows, returned_prob = (
        lax.all_to_all(produced[0], "ep", split_axis=0, concat_axis=0, tiled=True),
        lax.all_to_all(produced[1], "ep", split_axis=0, concat_axis=0, tiled=True),
    )
    extras = produced[2:]
    back_gate, back_up, hidden, scaled, flat_x = [
        member.reshape(-1, member.shape[-1]) for member in extras
    ]
    grad_tokens = returned_rows.reshape(slots_all, width)[target]
    grad_prob = returned_prob.reshape(slots_all)[target][:, None]
    contract_rows = (((0,), (0,)), ((), ()))
    term_gate = lax.dot_general(
        flat_x, back_gate, contract_rows, preferred_element_type=jnp.float32
    )[None]
    term_up = lax.dot_general(flat_x, back_up, contract_rows, preferred_element_type=jnp.float32)[
        None
    ]
    term_down = lax.dot_general(scaled, hidden, contract_rows, preferred_element_type=jnp.float32)[
        None
    ]
    grad_gate, grad_up, grad_down = (
        lax.psum_scatter(
            term_gate.astype(jnp.bfloat16), "group", scatter_dimension=1, tiled=True
        ).astype(jnp.float32),
        lax.psum_scatter(
            term_up.astype(jnp.bfloat16), "group", scatter_dimension=1, tiled=True
        ).astype(jnp.float32),
        lax.psum_scatter(
            term_down.astype(jnp.bfloat16), "group", scatter_dimension=1, tiled=True
        ).astype(jnp.float32),
    )
    return (grad_tokens, grad_prob, grad_gate, grad_up, grad_down)


def solution(mesh):
    in_specs = (
        P(("group", "ep"), None),
        P(("group", "ep"), None),
        P(("group", "ep"), None),
        P(("group", "ep"), None),
        P("ep", None, None),
        P("ep", None, None),
        P("ep", None, None),
    )
    out_specs = (
        P(("group", "ep"), None),
        P(("group", "ep"), None),
        P("ep", "group", None),
        P("ep", "group", None),
        P("ep", "group", None),
    )
    return jax.shard_map(
        per_device, mesh=mesh, in_specs=in_specs, out_specs=out_specs, check_vma=False
    )
```

profile of v0, /device:TPU:1, one launch (start us, length us, event | category | flops | bytes accessed | tf_op | source)
XLA Modules:
  0.0 699.2 jit_solution(14009348587754330259)
XLA Ops:
  7.2 0.9 fusion.23
  8.1 0.2 reduce_window_sum.11
  8.2 0.8 select_reduce_fusion
  9.1 0.7 fusion.24
  9.7 1.5 scatter_custom_fusion
  11.2 0.7 all_to_all.25
  12.0 29.3 %all-to-all-start = ((bf16[32,1,5]{2,1,0:T(2,128)(2,1)}), bf16[32,1,5]{2,1,0:T(2,128)(2,1)S(1)}, u32[]{:S(2)}, u32[]{:S(2)}) async-start(bf16[32,1,5]{2,1,0:T(2,128)(2,1)} %all_to_all.25), calls=%async_computation | async-start | bytes 32768 | tf_op jit(solution)/shard_map/all_to_all | solution.py:80
  41.2 2.1 scatter_custom_fusion.1
  43.3 1.2 reshape.74
  44.6 17.9 %all-to-all-done = bf16[32,1,5]{2,1,0:T(2,128)(2,1)S(1)} async-done(((bf16[32,1,5]{2,1,0:T(2,128)(2,1)}), bf16[32,1,5]{2,1,0:T(2,128)(2,1)S(1)}, u32[]{:S(2)}, u32[]{:S(2)}) %all-to-all-start) | async-done | bytes 352 | tf_op jit(solution)/shard_map/all_to_all | solution.py:80
  62.4 3.9 all-to-all-start.1
  66.4 2.7 scatter_custom_fusion.2
  69.1 2.3 reshape.75
  71.4 100.4 %all-to-all-done.1 = bf16[32,5,2048]{2,1,0:T(8,128)(2,1)S(1)} async-done(((bf16[32,5,2048]{2,1,0:T(8,128)(2,1)}), bf16[32,5,2048]{2,1,0:T(8,128)(2,1)S(1)}, u32[]{:S(2)}, u32[]{:S(2)}) %all-to-all-start.1) | async-done | bytes 655392 | tf_op jit(solution)/shard_map/all_to_all | solution.py:79
  171.8 7.2 %all-to-all-start.2 = ((bf16[32,5,2048]{2,1,0:T(8,128)(2,1)}), bf16[32,5,2048]{2,1,0:T(8,128)(2,1)}, u32[]{:S(2)}, u32[]{:S(2)}) async-start(bf16[32,5,2048]{2,1,0:T(8,128)(2,1)} %reshape.75), calls=%async_computation.2 | async-start | bytes 2097152 | tf_op jit(solution)/shard_map/all_to_all | solution.py:78
  179.0 0.1 convert_reduce_fusion
  179.1 0.1 reshape.82
  179.2 1.2 multiply_convert_fusion
  180.4 2.2 convert_element_type.94
  182.6 101.5 %all-to-all-done.2 = bf16[32,5,2048]{2,1,0:T(8,128)(2,1)} async-done(((bf16[32,5,2048]{2,1,0:T(8,128)(2,1)}), bf16[32,5,2048]{2,1,0:T(8,128)(2,1)}, u32[]{:S(2)}, u32[]{:S(2)}) %all-to-all-start.2) | async-done | bytes 655392 | tf_op jit(solution)/shard_map/all_to_all | solution.py:78
  284.1 1.5 reshape.76
  285.6 2.4 fusion.6
  288.0 0.1 copy-done.4
  288.1 0.5 fusion.12
  288.6 1.4 multiply_convert_fusion.3
  289.9 1.4 reshape.81
  291.4 3.0 fusion.2
  294.5 3.2 fusion.1
  297.7 2.6 fusion.14
  300.4 0.7 convert_element_type.118
  301.1 7.0 all-to-all-start.4
  308.1 2.5 fusion.4
  310.6 0.8 fusion.3
  311.4 1.2 reshape.77
  312.7 16.5 %all-to-all-done.4 = bf16[32,1,5]{2,1,0:T(2,128)(2,1)S(1)} async-done(((bf16[32,1,5]{2,1,0:T(2,128)(2,1)}), bf16[32,1,5]{2,1,0:T(2,128)(2,1)S(1)}, u32[]{:S(2)}, u32[]{:S(2)}) %all-to-all-start.4) | async-done | bytes 352 | tf_op jit(solution)/shard_map/all_to_all | solution.py:85
  329.2 5.0 all-to-all-start.3
  334.3 2.1 fusion
  336.4 0.1 reduce
  336.4 0.1 reshape.79
  336.6 1.7 gather_fusion.1
  338.3 73.9 %reduce-scatter.8.cloned.1.call-done = bf16[1,64,512]{2,1,0:T(8,128)(2,1)} async-done(((bf16[1,2048,512]{2,1,0:T(8,128)(2,1)}), bf16[1,64,512]{2,1,0:T(8,128)(2,1)}) %reduce-scatter.8.cloned.1.call-update) | async-done | bytes 65552 | tf_op jit(solution)/shard_map/reduce_scatter | solution.py:110
  412.2 1.5 convert_element_type.114
  413.7 136.1 %reduce-scatter.6.cloned.1.call-done = bf16[1,64,512]{2,1,0:T(8,128)(2,1)} async-done(((bf16[1,2048,512]{2,1,0:T(8,128)(2,1)}), bf16[1,64,512]{2,1,0:T(8,128)(2,1)}) %reduce-scatter.6.cloned.1.call-update) | async-done | bytes 65552 | tf_op jit(solution)/shard_map/reduce_scatter | solution.py:107
  549.9 1.5 convert_element_type.108
  551.4 136.6 %reduce-scatter.4.cloned.1.call-done = bf16[1,64,512]{2,1,0:T(8,128)(2,1)} async-done(((bf16[1,2048,512]{2,1,0:T(8,128)(2,1)}), bf16[1,64,512]{2,1,0:T(8,128)(2,1)}) %reduce-scatter.4.cloned.1.call-update) | async-done | bytes 65552 | tf_op jit(solution)/shard_map/reduce_scatter | solution.py:104
  687.9 1.5 convert_element_type.105
  689.4 1.5 reshape.78
  690.9 1.7 gather_fusion
  (24 shorter events, 0.2 us)
Async XLA Ops:
  7.2 281.4 %copy-start = (bf16[1,2048,512]{2,1,0:T(8,128)(2,1)S(1)}, bf16[1,2048,512]{2,1,0:T(8,128)(2,1)}, u32[]{:S(2)}) copy-start(bf16[1,2048,512]{2,1,0:T(8,128)(2,1)} %param.12) | copy-start | bytes 6291460
  12.0 50.5 %all-to-all-start = ((bf16[32,1,5]{2,1,0:T(2,128)(2,1)}), bf16[32,1,5]{2,1,0:T(2,128)(2,1)S(1)}, u32[]{:S(2)}, u32[]{:S(2)}) async-start(bf16[32,1,5]{2,1,0:T(2,128)(2,1)} %all_to_all.25), calls=%async_computation | async-start | bytes 32768 | tf_op jit(solution)/shard_map/all_to_all | solution.py:80
  62.4 109.3 %all-to-all-start.1 = ((bf16[32,5,2048]{2,1,0:T(8,128)(2,1)}), bf16[32,5,2048]{2,1,0:T(8,128)(2,1)S(1)}, u32[]{:S(2)}, u32[]{:S(2)}) async-start(bf16[32,5,2048]{2,1,0:T(8,128)(2,1)} %reshape.74), calls=%async_computation.1 | async-start | bytes 2097152 | tf_op jit(solution)/shard_map/all_to_all | solution.py:79
  171.8 8.7 %copy-start.3 = (bf16[32,5,2048]{2,1,0:T(8,128)(2,1)}, bf16[32,5,2048]{2,1,0:T(8,128)(2,1)S(1)}, u32[]{:S(2)}) copy-start(bf16[32,5,2048]{2,1,0:T(8,128)(2,1)S(1)} %all-to-all-done.1) | copy-start | bytes 1966084
  171.8 112.4 %all-to-all-start.2 = ((bf16[32,5,2048]{2,1,0:T(8,128)(2,1)}), bf16[32,5,2048]{2,1,0:T(8,128)(2,1)}, u32[]{:S(2)}, u32[]{:S(2)}) async-start(bf16[32,5,2048]{2,1,0:T(8,128)(2,1)} %reshape.75), calls=%async_computation.2 | async-start | bytes 2097152 | tf_op jit(solution)/shard_map/all_to_all | solution.py:78
  179.0 233.2 %reduce-scatter.8.cloned.1.call-start = ((), (), s32[]{:S(2)}) async-start(), calls=%async_computation.10 | async-start | bytes 2162688 | tf_op jit(solution)/shard_map/reduce_scatter | solution.py:110
  182.6 105.3 %copy-start.5 = (bf16[160,2048]{1,0:T(8,128)(2,1)S(1)}, bf16[160,2048]{1,0:T(8,128)(2,1)}, u32[]{:S(2)}) copy-start(bf16[160,2048]{1,0:T(8,128)(2,1)} %convert_element_type.94) | copy-start | bytes 1966084
  285.6 3.0 copy-start.1
  285.6 2.5 copy-start.4
  294.4 255.4 %reduce-scatter.6.cloned.1.call-start = ((), (), s32[]{:S(2)}) async-start(), calls=%async_computation.9 | async-start | bytes 2162688 | tf_op jit(solution)/shard_map/reduce_scatter | solution.py:107
  300.4 10.2 %copy-start.7 = (bf16[160,512]{1,0:T(8,128)(2,1)S(1)}, bf16[160,512]{1,0:T(8,128)(2,1)}, u32[]{:S(2)}) copy-start(bf16[160,512]{1,0:T(8,128)(2,1)} %get-tuple-element.7) | copy-start | bytes 491524
  301.1 28.1 %all-to-all-start.4 = ((bf16[32,1,5]{2,1,0:T(2,128)(2,1)}), bf16[32,1,5]{2,1,0:T(2,128)(2,1)S(1)}, u32[]{:S(2)}, u32[]{:S(2)}) async-start(bf16[32,1,5]{2,1,0:T(2,128)(2,1)} %convert_element_type.118), calls=%async_computation.4 | async-start | bytes 32768 | tf_op jit(solution)/shard_map/all_to_all | solution.py:85
  311.4 22.8 %copy-start.2 = (bf16[160,2048]{1,0:T(8,128)(2,1)S(1)}, bf16[160,2048]{1,0:T(8,128)(2,1)}, u32[]{:S(2)}) copy-start(bf16[160,2048]{1,0:T(8,128)(2,1)} %copy-done.1) | copy-start | bytes 1966084
  312.7 21.6 %copy-start.6 = (bf16[160,512]{1,0:T(8,128)(2,1)S(1)}, bf16[160,512]{1,0:T(8,128)(2,1)}, u32[]{:S(2)}) copy-start(bf16[160,512]{1,0:T(8,128)(2,1)} %get-tuple-element.6) | copy-start | bytes 491524
  329.2 360.2 %all-to-all-start.3 = ((bf16[32,5,2048]{2,1,0:T(8,128)(2,1)}), bf16[32,5,2048]{2,1,0:T(8,128)(2,1)}, u32[]{:S(2)}, u32[]{:S(2)}) async-start(bf16[32,5,2048]{2,1,0:T(8,128)(2,1)} %reshape.77), calls=%async_computation.3 | async-start | bytes 2097152 | tf_op jit(solution)/shard_map/all_to_all | solution.py:84
  334.2 353.7 %reduce-scatter.4.cloned.1.call-start = ((), (), s32[]{:S(2)}) async-start(), calls=%async_computation.8 | async-start | bytes 2162688 | tf_op jit(solution)/shard_map/reduce_scatter | solution.py:104
Sparse Core Ops, SparseCore 0:
  294.6 117.6 reduce-scatter.7
  417.8 132.0 reduce-scatter.5
  555.4 132.4 reduce-scatter.3
where the time goes:
time: 701 us; the launch traced here: 699 us
  waiting for transfers between devices  583 us (83%)
  starting transfers between devices  52.5 us (7%)
  local copies, waits for them, and re-layouts  22.8 us (3%)
  matrix products  18.5 us (3%)
  between operations  14 us (2%)
  other arithmetic  8.44 us (1%)
    reduce_scatter x1, waiting for transfers between devices, per_device(): lax.psum_scatter(term_gate.astype(jnp.bfloat16), 'group', scatter_dimensi...  137 us
    reduce_scatter x1, waiting for transfers between devices, per_device(): lax.psum_scatter(term_up.astype(jnp.bfloat16), 'group', scatter_dimension...  136 us
    all_to_all x1, waiting for transfers between devices, per_device(): lax.all_to_all(send_x, 'ep', split_axis=0, concat_axis=0, tiled=True)  101 us
    all_to_all x1, waiting for transfers between devices, per_device(): lax.all_to_all(send_dy, 'ep', split_axis=0, concat_axis=0, tiled=True)  100 us
    reduce_scatter x1, waiting for transfers between devices, per_device(): lax.psum_scatter(term_down.astype(jnp.bfloat16), 'group', scatter_dimensi...  73.9 us
    all_to_all x1, starting transfers between devices, per_device(): lax.all_to_all(send_p, 'ep', split_axis=0, concat_axis=0, tiled=True)  29.3 us
    all_to_all x1, waiting for transfers between devices, per_device(): lax.all_to_all(send_p, 'ep', split_axis=0, concat_axis=0, tiled=True)  17.9 us
    all_to_all x1, waiting for transfers between devices, per_device(): lax.all_to_all(produced[1], 'ep', split_axis=0, concat_axis=0, tiled=True)  16.5 us
  transfers between devices with their start and end apart: 8, of which 7 were waited for; matrix products, arithmetic and copies ran while one was open for 5% of the time, Pallas kernels for 0%

commit v1 on v0

v1 whole, which is shorter than its diff:
```python
import functools

import jax
import jax.numpy as jnp
from jax import lax
from jax.experimental import pallas as pl
from jax.experimental.pallas import tpu as pltpu
from jax.sharding import PartitionSpec as P

MESH = pl.DeviceIdType.MESH
F32 = jnp.float32
BF16 = jnp.bfloat16
LANES = 128


def ring_steps(n, body):
    half = n // 2
    body(half)

    def pair(i, carry):
        body(half - i)
        body(half + i)
        return carry

    lax.fori_loop(1, half, pair, 0)


def iota(shape, dim):
    return lax.broadcasted_iota(jnp.int32, shape, dim).astype(F32)


def one_hot(mask):
    return jnp.where(mask, 1.0, 0.0)


def kernel(
    cap,
    n_ep,
    n_grp,
    x_ref,
    dy_ref,
    p_ref,
    ids_ref,
    ids_row_ref,
    wg_hbm,
    wu_hbm,
    wd_hbm,
    gt_ref,
    gp_ref,
    gg_ref,
    gu_ref,
    gd_ref,
    wg,
    wu,
    wd,
    wide,
    xs,
    ds,
    xr,
    dr,
    x2,
    d2,
    ys,
    yr,
    ps,
    pr,
    part,
    held,
    total,
    landed,
    w_sem,
    x_sems,
    d_sems,
    y_sems,
    p_sems,
    pair_sems,
    plane_sems,
):
    me = lax.axis_index("ep")
    grp = lax.axis_index("group")
    core = lax.rem(grp, 2)
    chip = grp // 2
    n_chip = n_grp // 2
    tok, width = x_ref.shape
    slots = n_ep * cap
    blocks = width // LANES
    rows = width // n_grp

    barrier = pltpu.get_barrier_semaphore()

    def greet_ring(k, carry):
        pl.semaphore_signal(
            barrier, inc=1, device_id={"ep": lax.rem(me + k, n_ep)}, device_id_type=MESH
        )
        return carry

    def greet_plane(k, carry):
        pl.semaphore_signal(
            barrier,
            inc=1,
            device_id={"group": lax.rem(chip + k, n_chip) * 2 + core},
            device_id_type=MESH,
        )
        return carry

    sibling = {"group": chip * 2 + 1 - core}
    lax.fori_loop(1, n_ep, greet_ring, 0)
    lax.fori_loop(1, n_chip, greet_plane, 0)
    pl.semaphore_signal(barrier, inc=1, device_id=sibling, device_id_type=MESH)

    weight_copies = [
        pltpu.make_async_copy(src.at[0], dst, w_sem.at[i])
        for i, (src, dst) in enumerate(((wg_hbm, wg), (wu_hbm, wu), (wd_hbm, wd)))
    ]
    for copy in weight_copies:
        copy.start()

    ids_col = ids_ref[...].astype(F32)
    ids_row = ids_row_ref[...].astype(F32)
    hits = one_hot(ids_col == iota((tok, n_ep), 1))
    earlier = one_hot(iota((tok, tok), 1) < iota((tok, tok), 0))
    before = jnp.dot(earlier.astype(BF16), hits.astype(BF16), preferred_element_type=F32)
    rank_col = jnp.sum(before * hits, axis=1, keepdims=True)
    target_col = ids_col * cap + rank_col
    hits_t = one_hot(ids_row == iota((n_ep, tok), 0))
    later = one_hot(iota((tok, tok), 0) < iota((tok, tok), 1))
    before_t = jnp.dot(hits_t.astype(BF16), later.astype(BF16), preferred_element_type=F32)
    rank_row = jnp.sum(before_t * hits_t, axis=0, keepdims=True)
    target_row = ids_row * cap + rank_row
    place = one_hot(target_row == iota((slots, tok), 0)).astype(BF16)
    take = one_hot(target_col == iota((tok, slots), 1)).astype(BF16)

    def spread(columns, block):
        wide[pl.ds(block, slots, stride=blocks), :] = columns

    def pack(dst):
        dst[...] = wide[...].reshape(slots, blocks, LANES).astype(BF16)

    def unpack(src):
        wide[...] = src[...].astype(F32).reshape(slots * blocks, LANES)

    def column(block):
        return wide[pl.ds(block, slots, stride=blocks), :].astype(BF16)

    def ring_copy(src, dst, sems, k, size):
        to = lax.rem(me + k, n_ep)
        return pltpu.make_async_remote_copy(
            src_ref=src.at[pl.ds(to * size, size)],
            dst_ref=dst.at[pl.ds(me * size, size)],
            send_sem=sems.at[0, k],
            recv_sem=sems.at[1, k],
            device_id={"ep": to},
            device_id_type=MESH,
        )

    def wait_ring(src, dst, sems, size):
        def one(k, carry):
            ring_copy(src, dst, sems, k, size).wait()
            return carry

        lax.fori_loop(1, n_ep, one, 0)

    step = 2 * LANES
    for j in range(width // step):
        placed = jnp.dot(place, x_ref[:, j * step : (j + 1) * step], preferred_element_type=F32)
        spread(placed[:, :LANES], 2 * j)
        spread(placed[:, LANES:], 2 * j + 1)
    pack(xs)
    xr[pl.ds(me * cap, cap)] = xs[pl.ds(me * cap, cap)]

    pl.semaphore_wait(barrier, n_ep - 1 + n_chip - 1 + 1)
    ring_steps(n_ep, lambda k: ring_copy(xs, xr, x_sems, k, cap).start())

    prob = p_ref[...].astype(F32)
    for j in range(width // step):
        scaled = (prob * dy_ref[:, j * step : (j + 1) * step].astype(F32)).astype(BF16)
        placed = jnp.dot(place, scaled, preferred_element_type=F32)
        spread(placed[:, :LANES], 2 * j)
        spread(placed[:, LANES:], 2 * j + 1)
    pack(ds)
    dr[pl.ds(me * cap, cap)] = ds[pl.ds(me * cap, cap)]
    ring_steps(n_ep, lambda k: ring_copy(ds, dr, d_sems, k, cap).start())

    for copy in weight_copies:
        copy.wait()
    wait_ring(xs, xr, x_sems, cap)
    unpack(xr)
    for b in range(blocks):
        x2[:, b * LANES : (b + 1) * LANES] = column(b)
    gate_pre = jnp.dot(x2[...], wg[...], preferred_element_type=F32)
    up_pre = jnp.dot(x2[...], wu[...], preferred_element_type=F32)
    sig = jax.nn.sigmoid(gate_pre)
    active = gate_pre * sig
    hidden = (active * up_pre).astype(BF16)
    gate_slope = up_pre * sig * (1.0 + gate_pre * (1.0 - sig))

    wait_ring(ds, dr, d_sems, cap)
    unpack(dr)
    for b in range(blocks):
        d2[:, b * LANES : (b + 1) * LANES] = column(b)
    back_hidden = jnp.dot(d2[...], wd[...], preferred_element_type=F32)
    back_gate = (back_hidden * gate_slope).astype(BF16)
    back_up = (back_hidden * active).astype(BF16)
    contract_h = (((1,), (1,)), ((), ()))
    for j in range(width // step):
        span = slice(j * step, (j + 1) * step)
        back = lax.dot_general(back_gate, wg[span, :], contract_h, preferred_element_type=F32)
        back += lax.dot_general(back_up, wu[span, :], contract_h, preferred_element_type=F32)
        spread(back[:, :LANES], 2 * j)
        spread(back[:, LANES:], 2 * j + 1)
    pack(ys)
    yr[pl.ds(me * cap, cap)] = ys[pl.ds(me * cap, cap)]
    ring_steps(n_ep, lambda k: ring_copy(ys, yr, y_sems, k, cap).start())

    weighted = jnp.sum(hidden.astype(F32) * back_hidden, axis=1, keepdims=True)
    slot_of = iota((slots, LANES), 0)
    lane = iota((slots, LANES), 1)
    source = jnp.floor((slot_of + 0.5) * (1.0 / cap))
    by_lane = weighted * one_hot(slot_of - source * cap == lane)
    row_iota = iota((n_ep, slots), 0)
    offset = iota((n_ep, slots), 1) - row_iota * cap
    collect = one_hot((offset >= 0.0) & (offset < cap))
    prob_rows = jnp.dot(
        collect, by_lane, precision=lax.Precision.HIGHEST, preferred_element_type=F32
    )
    ps[...] = prob_rows.reshape(n_ep, 1, LANES)
    pr[pl.ds(me, 1)] = ps[pl.ds(me, 1)]
    ring_steps(n_ep, lambda k: ring_copy(ps, pr, p_sems, k, 1).start())

    contract_rows = (((0,), (0,)), ((), ()))

    def pair_copy(c):
        return pltpu.make_async_remote_copy(
            src_ref=part.at[1 - core, c],
            dst_ref=held.at[c],
            send_sem=pair_sems.at[0, c],
            recv_sem=pair_sems.at[1, c],
            device_id=sibling,
            device_id_type=MESH,
        )

    def plane_copy(k):
        to = lax.rem(chip + k, n_chip)
        return pltpu.make_async_remote_copy(
            src_ref=total.at[to],
            dst_ref=landed.at[chip],
            send_sem=plane_sems.at[0, k],
            recv_sem=plane_sems.at[1, k],
            device_id={"group": to * 2 + core},
            device_id_type=MESH,
        )

    def partials(k, carry):
        c = lax.rem(chip + k, n_chip)
        span = pl.ds(pl.multiple_of(c * 2 * rows, 2 * rows), 2 * rows)
        for m, (left, right) in enumerate(((x2, back_gate), (x2, back_up), (d2, hidden))):
            term = lax.dot_general(left[:, span], right, contract_rows, preferred_element_type=F32)
            part[0, c, m] = term[:rows].astype(BF16)
            part[1, c, m] = term[rows:].astype(BF16)
        pair_copy(c).start()
        return carry

    lax.fori_loop(1, n_chip + 1, partials, 0)

    def add_pair(c):
        pair_copy(c).wait()
        total[c] = (part[core, c].astype(F32) + held[c].astype(F32)).astype(BF16)

    def pair_sums(k, carry):
        add_pair(lax.rem(chip + k, n_chip))
        plane_copy(k).start()
        return carry

    lax.fori_loop(1, n_chip, pair_sums, 0)
    add_pair(chip)

    def wait_plane(k, carry):
        plane_copy(k).wait()
        return carry

    landed[pl.ds(chip, 1)] = total[pl.ds(chip, 1)]
    lax.fori_loop(1, n_chip, wait_plane, 0)
    for m, out in enumerate((gg_ref, gu_ref, gd_ref)):
        acc = landed[0, m].astype(F32)
        for c in range(1, n_chip):
            acc += landed[c, m].astype(F32)
        out[0] = acc

    wait_ring(ps, pr, p_sems, 1)
    table = pr[...].reshape(n_ep, LANES)
    mine = jnp.dot(hits, table, precision=lax.Precision.HIGHEST, preferred_element_type=F32)
    picked = jnp.sum(
        mine * one_hot(rank_col == iota((tok, LANES), 1)), axis=1, keepdims=True
    )
    gp_ref[...] = (picked / prob).astype(BF16)

    wait_ring(ys, yr, y_sems, cap)
    unpack(yr)
    for b in range(blocks):
        gt_ref[:, b * LANES : (b + 1) * LANES] = jnp.dot(
            take, column(b), preferred_element_type=F32
        ).astype(BF16)


def per_device(tokens, cotangent, gate_prob, expert_ids, gate_weight, up_weight, down_weight):
    n_ep = lax.axis_size("ep")
    n_grp = lax.axis_size("group")
    tok, width = tokens.shape
    hid = gate_weight.shape[-1]
    cap = tok // n_ep + max(1, tok // (4 * n_ep))
    slots = n_ep * cap
    blocks = width // LANES
    rows = width // n_grp
    n_chip = n_grp // 2
    vmem = pl.BlockSpec(memory_space=pltpu.VMEM)
    hbm = pl.BlockSpec(memory_space=pl.ANY)
    tiled = pltpu.VMEM((slots, blocks, LANES), BF16)
    flat = pltpu.VMEM((slots, width), BF16)
    probs = pltpu.VMEM((n_ep, 1, LANES), F32)
    slices = pltpu.VMEM((n_chip, 3, rows, hid), BF16)
    ring_sems = pltpu.SemaphoreType.DMA((2, n_ep))
    plane_sems = pltpu.SemaphoreType.DMA((2, n_chip))
    grad = jax.ShapeDtypeStruct((1, rows, hid), F32)
    return pl.pallas_call(
        functools.partial(kernel, cap, n_ep, n_grp),
        out_shape=(
            jax.ShapeDtypeStruct((tok, width), BF16),
            jax.ShapeDtypeStruct((tok, 1), BF16),
            grad,
            grad,
            grad,
        ),
        in_specs=[vmem] * 5 + [hbm] * 3,
        out_specs=[vmem] * 5,
        scratch_shapes=[
            pltpu.VMEM((width, hid), BF16),
            pltpu.VMEM((width, hid), BF16),
            pltpu.VMEM((width, hid), BF16),
            pltpu.VMEM((slots * blocks, LANES), F32),
            tiled,
            tiled,
            tiled,
            tiled,
            flat,
            flat,
            tiled,
            tiled,
            probs,
            probs,
            pltpu.VMEM((2, n_chip, 3, rows, hid), BF16),
            slices,
            slices,
            slices,
            pltpu.SemaphoreType.DMA((3,)),
            ring_sems,
            ring_sems,
            ring_sems,
            ring_sems,
            plane_sems,
            plane_sems,
        ],
        compiler_params=pltpu.CompilerParams(
            collective_id=0, has_side_effects=True, vmem_limit_bytes=56 << 20
        ),
    )(
        tokens,
        cotangent,
        gate_prob,
        expert_ids,
        expert_ids.reshape(1, tok),
        gate_weight,
        up_weight,
        down_weight,
    )


def solution(mesh):
    in_specs = (
        P(("group", "ep"), None),
        P(("group", "ep"), None),
        P(("group", "ep"), None),
        P(("group", "ep"), None),
        P("ep", None, None),
        P("ep", None, None),
        P("ep", None, None),
    )
    out_specs = (
        P(("group", "ep"), None),
        P(("group", "ep"), None),
        P("ep", "group", None),
        P("ep", "group", None),
        P("ep", "group", None),
    )
    return jax.shard_map(
        per_device, mesh=mesh, in_specs=in_specs, out_specs=out_specs, check_vma=False
    )
```

time: 701 us -> 227 us (0.32)
  waiting for transfers between devices: 583 us -> 0 us
  Pallas kernels: 0 us -> 215 us
  starting transfers between devices: 52.5 us -> 0 us
  matrix products: 18.5 us -> 0 us
  between operations: 14 us -> 0.64 us
  local copies, waits for them, and re-layouts: 22.8 us -> 10.7 us
  other arithmetic: 8.44 us -> 0 us
    reduce_scatter x3 -> x0, waiting for transfers between devices: 347 us -> none  [the longest x1 137 us: per_device(): lax.psum_scatter(term_gate.astype(jnp.bfloat16), 'group', scatter_dimensi...]
    all_to_all x5 -> x0, waiting for transfers between devices: 236 us -> none  [the longest x1 101 us: per_device(): lax.all_to_all(send_x, 'ep', split_axis=0, concat_axis=0, tiled=True)]
    pallas_call x0 -> x1, Pallas kernels: none -> 215 us  [per_device(): pl.pallas_call(functools.partial(kernel, cap, n_ep, n_grp), out_shape=(ja...]
    all_to_all x5 -> x0, starting transfers between devices: 52.4 us -> none  [the longest x1 29.3 us: per_device(): lax.all_to_all(send_p, 'ep', split_axis=0, concat_axis=0, tiled=True)]
    dot_general x9 -> x0, matrix products: 18.5 us -> none  [the longest x1 3.22 us: per_device(): lax.dot_general(flat_x, back_up, contract_rows, preferred_element_type=jn...]
    unnamed x16 -> x6, local copies, waits for them, and re-layouts: 0.1 us -> 9.35 us
    reshape x6 -> x0, local copies, waits for them, and re-layouts: 7.77 us -> none  [the longest x1 2.27 us: per_device(): send_x = jnp.zeros((slots_all, width), jnp.bfloat16).at[target].set(token...]
  transfers between devices with their start and end apart: 8 -> 0, of which waited for: 7 -> 0; matrix products, arithmetic and copies ran while one was open for 5% -> 0% of each run, Pallas kernels for 0% -> 0%
where the time goes in v1:
time: 227 us
  Pallas kernels  215 us (95%)
  local copies, waits for them, and re-layouts  10.7 us (5%)
    pallas_call x1, Pallas kernels, per_device(): pl.pallas_call(functools.partial(kernel, cap, n_ep, n_grp), out_shape=(ja...  215 us
    unnamed x6, local copies, waits for them, and re-layouts  9.35 us

profile of v1, /device:TPU:1, one launch (start us, length us, event | category | flops | bytes accessed | tf_op | source)
XLA Modules:
  0.0 226.7 jit_solution(10546740487550884496)
XLA Ops:
  0.6 1.4 copy.12.p_ref
  2.0 1.4 copy.13.ids_ref
  3.4 215.4 %shard_map.110 = (bf16[128,2048]{1,0:T(8,128)(2,1)}, bf16[128,1]{1,0:T(8,128)(2,1)}, f32[1,64,512]{2,1,0:T(8,128)}, f32[1,64,512]{2,1,0:T(8,128)}, f32[1,64,512]{2,1,0:T(8,128)}) custom-call(bf16[128,2048]{1,0:T(8,128)(2,1)} %x_ref.1, bf16[128,2048]{1,0:T(8,128)(2,1)} %dy_ref.1, bf16[128,1]{1,0:T(8,128)(2,1)} %copy.12.p_ref, s32[128,1]{1,0:T(8,128)} %copy.13.ids_ref, ...), custom_call_target="tpu_custom_call" | custom-call | tf_op jit(solution)/shard_map/pallas_call | solution.py:324
  218.8 1.4 copy.14
  220.2 1.9 copy.19
  222.0 1.6 copy.20
  223.6 1.6 copy.21
  225.2 1.6 copy.22

commit v2 on v1

v2 whole, which is shorter than its diff:
```python
import functools
import math

import jax
import jax.numpy as jnp
from jax import lax
from jax.experimental import pallas as pl
from jax.experimental.pallas import tpu as pltpu
from jax.sharding import PartitionSpec as P

MESH = pl.DeviceIdType.MESH
F32 = jnp.float32
BF16 = jnp.bfloat16
LANES = 128


def batch_steps(n, batch, body):
    half, quarter = n // 2, n // 4
    body(half if batch == 0 else quarter)

    def pair(i, carry):
        near = quarter - i
        body(half - i if batch == 0 else near)
        body(half + i if batch == 0 else n - near)
        return carry

    lax.fori_loop(1, quarter, pair, 0)
    if batch == 0:
        body(3 * quarter)


def iota(shape, dim):
    return lax.broadcasted_iota(jnp.int32, shape, dim).astype(F32)


def one_hot(mask):
    return jnp.where(mask, 1.0, 0.0)


def kernel(
    cap,
    n_ep,
    side,
    x_ref,
    dy_ref,
    p_ref,
    ids_ref,
    wg_hbm,
    wu_hbm,
    wd_hbm,
    gt_ref,
    gp_ref,
    gg_ref,
    gu_ref,
    gd_ref,
    wg,
    wu,
    wd,
    wide,
    scaled,
    xs,
    ds,
    xr,
    dr,
    x2,
    d2,
    bg,
    bu,
    ys,
    yr,
    ps,
    pr,
    part,
    held,
    mid,
    mid_in,
    last,
    last_in,
    w_sem,
    x_sems,
    d_sems,
    y_sems,
    p_sems,
    pair_sems,
    mid_sems,
    last_sems,
):
    me = lax.axis_index("ep")
    grp = lax.axis_index("group")
    core = lax.rem(grp, 2)
    chip = grp // 2
    n_chip = side * side
    at_y, at_x = chip // side, lax.rem(chip, side)
    tok, width = x_ref.shape
    slots = n_ep * cap
    blocks = width // LANES
    rows = width // (2 * n_chip)
    quarter = n_ep // 4
    some = slots // 2

    def on_plane(half, a, b):
        return {"group": ((b * side + a) if half == 0 else (a * side + b)) * 2 + core}

    own_a, own_b = (at_x, at_y), (at_y, at_x)
    sibling = {"group": chip * 2 + 1 - core}
    barrier = pltpu.get_barrier_semaphore()

    def greet(device):
        pl.semaphore_signal(barrier, inc=1, device_id=device, device_id_type=MESH)

    def greet_ring(k, carry):
        greet({"ep": lax.rem(me + k, n_ep)})
        return carry

    lax.fori_loop(1, n_ep, greet_ring, 0)
    for half in range(2):
        for k in range(1, side):
            greet(on_plane(half, lax.rem(own_a[half] + k, side), own_b[half]))
    greet(sibling)

    weight_copies = [
        pltpu.make_async_copy(src.at[0], dst, w_sem.at[i])
        for i, (src, dst) in enumerate(((wg_hbm, wg), (wu_hbm, wu), (wd_hbm, wd)))
    ]
    for copy in weight_copies:
        copy.start()

    turned = lax.rem(ids_ref[...] + (2 * n_ep - quarter - 1) - me, n_ep).astype(F32)
    hits_t = one_hot(turned == iota((n_ep, tok), 0))
    later = one_hot(iota((tok, tok), 0) < iota((tok, tok), 1))
    before_t = jnp.dot(hits_t.astype(BF16), later.astype(BF16), preferred_element_type=F32)
    rank_row = jnp.sum(before_t * hits_t, axis=0, keepdims=True)
    target_row = turned * cap + rank_row
    place = one_hot(target_row == iota((slots, tok), 0)).astype(BF16)
    diagonal = iota((tok, tok), 0) == iota((tok, tok), 1)

    def upright(row):
        return jnp.sum(jnp.where(diagonal, row, 0.0), axis=1, keepdims=True)

    step = 2 * LANES

    def spread(batch, columns, block):
        wide[pl.ds(batch * some * blocks + block, some, stride=blocks), :] = columns

    def tiles(batch):
        return slice(batch * some * blocks, (batch + 1) * some * blocks)

    def pack(batch, dst):
        dst[batch * some : (batch + 1) * some] = (
            wide[tiles(batch), :].reshape(some, blocks, LANES).astype(BF16)
        )

    def unpack(batch, src, dst):
        wide[tiles(batch), :] = (
            src[batch * some : (batch + 1) * some].astype(F32).reshape(some * blocks, LANES)
        )
        for b in range(blocks):
            dst[batch * some : (batch + 1) * some, b * LANES : (b + 1) * LANES] = wide[
                pl.ds(batch * some * blocks + b, some, stride=blocks), :
            ].astype(BF16)

    def sent_at(k):
        return lax.rem(k + n_ep - quarter - 1, n_ep)

    def got_at(k):
        return lax.rem(2 * n_ep - k - quarter, n_ep)

    def out_copy(src, dst, sems, k, size):
        return pltpu.make_async_remote_copy(
            src_ref=src.at[pl.ds(sent_at(k) * size, size)],
            dst_ref=dst.at[pl.ds(got_at(k) * size, size)],
            send_sem=sems.at[0, k],
            recv_sem=sems.at[1, k],
            device_id={"ep": lax.rem(me + k, n_ep)},
            device_id_type=MESH,
        )

    def home_copy(src, dst, sems, k, size):
        return pltpu.make_async_remote_copy(
            src_ref=src.at[pl.ds(got_at(k) * size, size)],
            dst_ref=dst.at[pl.ds(sent_at(k) * size, size)],
            send_sem=sems.at[0, k],
            recv_sem=sems.at[1, k],
            device_id={"ep": lax.rem(me + n_ep - k, n_ep)},
            device_id_type=MESH,
        )

    own_sent, own_got = n_ep - quarter - 1, n_ep - quarter

    def to_slots(batch, values, dst):
        chosen = place[batch * some : (batch + 1) * some]
        for j in range(width // step):
            span = slice(j * step, (j + 1) * step)
            placed = jnp.dot(chosen, values[:, span], preferred_element_type=F32)
            spread(batch, placed[:, :LANES], 2 * j)
            spread(batch, placed[:, LANES:], 2 * j + 1)
        pack(batch, dst)

    to_slots(0, x_ref, xs)
    pl.semaphore_wait(barrier, n_ep - 1 + 2 * (side - 1) + 1)
    batch_steps(n_ep, 0, lambda k: out_copy(xs, xr, x_sems, k, cap).start())
    to_slots(1, x_ref, xs)
    batch_steps(n_ep, 1, lambda k: out_copy(xs, xr, x_sems, k, cap).start())
    xr[own_got * cap : (own_got + 1) * cap] = xs[own_sent * cap : (own_sent + 1) * cap]

    prob_row = p_ref[...].astype(F32)
    prob = upright(prob_row)
    scaled[...] = (prob * dy_ref[...].astype(F32)).astype(BF16)
    for batch in range(2):
        to_slots(batch, scaled, ds)
        batch_steps(n_ep, batch, lambda k: out_copy(ds, dr, d_sems, k, cap).start())
    dr[own_got * cap : (own_got + 1) * cap] = ds[own_sent * cap : (own_sent + 1) * cap]

    for copy in weight_copies:
        copy.wait()
    for batch in range(2):
        batch_steps(n_ep, batch, lambda k: out_copy(xs, xr, x_sems, k, cap).wait())
        unpack(batch, xr, x2)
    gate_pre = jnp.dot(x2[...], wg[...], preferred_element_type=F32)
    up_pre = jnp.dot(x2[...], wu[...], preferred_element_type=F32)
    sig = jax.nn.sigmoid(gate_pre)
    active = gate_pre * sig
    hidden = (active * up_pre).astype(BF16)
    gate_slope = up_pre * sig * (1.0 + gate_pre * (1.0 - sig))

    slot_of = iota((some, LANES), 0)
    slot_lane = slot_of - jnp.floor((slot_of + 0.5) * (1.0 / cap)) * cap == iota((some, LANES), 1)
    offset = iota((n_ep // 2, some), 1) - iota((n_ep // 2, some), 0) * cap
    collect = one_hot((offset >= 0.0) & (offset < cap))
    contract_h = (((1,), (1,)), ((), ()))
    for batch in range(2):
        own = slice(batch * some, (batch + 1) * some)
        batch_steps(n_ep, batch, lambda k: out_copy(ds, dr, d_sems, k, cap).wait())
        unpack(batch, dr, d2)
        back_hidden = jnp.dot(d2[own, :], wd[...], preferred_element_type=F32)
        back_gate = (back_hidden * gate_slope[own]).astype(BF16)
        back_up = (back_hidden * active[own]).astype(BF16)
        bg[own, :] = back_gate
        bu[own, :] = back_up
        for j in range(width // step):
            span = slice(j * step, (j + 1) * step)
            back = lax.dot_general(back_gate, wg[span, :], contract_h, preferred_element_type=F32)
            back += lax.dot_general(back_up, wu[span, :], contract_h, preferred_element_type=F32)
            spread(batch, back[:, :LANES], 2 * j)
            spread(batch, back[:, LANES:], 2 * j + 1)
        pack(batch, ys)
        batch_steps(n_ep, batch, lambda k: home_copy(ys, yr, y_sems, k, cap).start())
        weighted = jnp.sum(hidden[own].astype(F32) * back_hidden, axis=1, keepdims=True)
        prob_rows = jnp.dot(
            collect,
            weighted * one_hot(slot_lane),
            precision=lax.Precision.HIGHEST,
            preferred_element_type=F32,
        )
        ps[batch * (n_ep // 2) : (batch + 1) * (n_ep // 2)] = prob_rows.reshape(
            n_ep // 2, 1, LANES
        )
    yr[own_sent * cap : (own_sent + 1) * cap] = ys[own_got * cap : (own_got + 1) * cap]
    pr[own_sent : own_sent + 1] = ps[own_got : own_got + 1]
    for batch in range(2):
        batch_steps(n_ep, batch, lambda k: home_copy(ps, pr, p_sems, k, 1).start())

    contract_rows = (((0,), (0,)), ((), ()))
    few = rows // 2

    def pair_copy(half, a, b):
        return pltpu.make_async_remote_copy(
            src_ref=part.at[1 - core, half, a, b],
            dst_ref=held.at[half, a, b],
            send_sem=pair_sems.at[0, half, a * side + b],
            recv_sem=pair_sems.at[1, half, a * side + b],
            device_id=sibling,
            device_id_type=MESH,
        )

    def partials(k, carry):
        c = lax.rem(chip + k, n_chip)
        c_y, c_x = c // side, lax.rem(c, side)
        span = pl.ds(pl.multiple_of(c * 2 * rows, 2 * rows), 2 * rows)
        for m, (left, right) in enumerate(((x2, bg[...]), (x2, bu[...]), (d2, hidden))):
            term = lax.dot_general(
                left[:, span], right, contract_rows, preferred_element_type=F32
            ).astype(BF16)
            for i in range(2):
                part[i, 0, c_x, c_y, m] = term[i * rows : i * rows + few]
                part[i, 1, c_y, c_x, m] = term[i * rows + few : (i + 1) * rows]
        pair_copy(0, c_x, c_y).start()
        pair_copy(1, c_y, c_x).start()
        return carry

    lax.fori_loop(1, n_chip + 1, partials, 0)

    def mid_copy(half, k):
        a = lax.rem(own_a[half] + k, side)
        return pltpu.make_async_remote_copy(
            src_ref=mid.at[half, a],
            dst_ref=mid_in.at[half, k],
            send_sem=mid_sems.at[0, half, k],
            recv_sem=mid_sems.at[1, half, k],
            device_id=on_plane(half, a, own_b[half]),
            device_id_type=MESH,
        )

    def last_copy(half, k):
        b = lax.rem(own_b[half] + k, side)
        return pltpu.make_async_remote_copy(
            src_ref=last.at[half, b],
            dst_ref=last_in.at[half, k],
            send_sem=last_sems.at[0, half, k],
            recv_sem=last_sems.at[1, half, k],
            device_id=on_plane(half, own_a[half], b),
            device_id_type=MESH,
        )

    for k in list(range(1, side)) + [0]:
        for half in range(2):
            a = lax.rem(own_a[half] + k, side)

            def add_pair(b, carry):
                pair_copy(half, a, b).wait()
                mid[half, a, b] = (
                    part[core, half, a, b].astype(F32) + held[half, a, b].astype(F32)
                ).astype(BF16)
                return carry

            lax.fori_loop(0, side, add_pair, 0)
            if k:
                mid_copy(half, k).start()

    for half in range(2):
        for k in range(1, side):
            mid_copy(half, k).wait()

        def add_mid(k, carry):
            b = lax.rem(own_b[half] + k, side)
            acc = mid[half, own_a[half], b].astype(F32)
            for i in range(1, side):
                acc += mid_in[half, i, b].astype(F32)
            last[half, b] = acc.astype(BF16)
            return carry

        lax.fori_loop(1, side + 1, add_mid, 0)
        for k in range(1, side):
            last_copy(half, k).start()

    for half in range(2):
        for k in range(1, side):
            last_copy(half, k).wait()
        for m, out in enumerate((gg_ref, gu_ref, gd_ref)):
            acc = last[half, own_b[half], m].astype(F32)
            for i in range(1, side):
                acc += last_in[half, i, m].astype(F32)
            out[0, half * few : (half + 1) * few] = acc

    hits = one_hot(upright(turned) == iota((tok, n_ep), 1))
    take = one_hot(upright(target_row) == iota((tok, slots), 1)).astype(BF16)
    lanes = one_hot(upright(rank_row) == iota((tok, LANES), 1))
    batch_steps(n_ep, 0, lambda k: home_copy(ys, yr, y_sems, k, cap).wait())
    unpack(0, yr, d2)
    for j in range(width // step):
        span = slice(j * step, (j + 1) * step)
        gt_ref[:, span] = jnp.dot(
            take[:, :some], d2[:some, span], preferred_element_type=F32
        ).astype(BF16)
    for batch in range(2):
        batch_steps(n_ep, batch, lambda k: home_copy(ps, pr, p_sems, k, 1).wait())
    table = pr[...].reshape(n_ep, LANES)
    mine = jnp.dot(hits, table, precision=lax.Precision.HIGHEST, preferred_element_type=F32)
    picked = jnp.sum(mine * lanes, axis=1, keepdims=True)
    grad_prob = jnp.sum(jnp.where(diagonal, picked, 0.0), axis=0, keepdims=True) / prob_row
    gp_ref[...] = grad_prob.astype(BF16)
    batch_steps(n_ep, 1, lambda k: home_copy(ys, yr, y_sems, k, cap).wait())
    unpack(1, yr, d2)
    for j in range(width // step):
        span = slice(j * step, (j + 1) * step)
        near = jnp.dot(take[:, some:], d2[some:, span], preferred_element_type=F32)
        gt_ref[:, span] = (gt_ref[:, span].astype(F32) + near).astype(BF16)


def hand_on(*refs):
    count = len(refs) // 2
    for src, dst in zip(refs[:count], refs[count:]):
        dst[...] = src[...]


def per_device(tokens, cotangent, gate_prob, expert_ids, gate_weight, up_weight, down_weight):
    n_ep = lax.axis_size("ep")
    n_grp = lax.axis_size("group")
    tok, width = tokens.shape
    hid = gate_weight.shape[-1]
    cap = tok // n_ep + max(1, tok // (4 * n_ep))
    slots = n_ep * cap
    blocks = width // LANES
    rows = width // n_grp
    side = math.isqrt(n_grp // 2)
    vmem = pl.BlockSpec(memory_space=pltpu.VMEM)
    hbm = pl.BlockSpec(memory_space=pl.ANY)
    weight = pltpu.VMEM((width, hid), BF16)
    tiled = pltpu.VMEM((slots, blocks, LANES), BF16)
    flat = pltpu.VMEM((slots, width), BF16)
    narrow = pltpu.VMEM((slots, hid), BF16)
    probs = pltpu.VMEM((n_ep, 1, LANES), F32)
    slices = (side, 3, rows // 2, hid)
    squares = pltpu.VMEM((2, side) + slices, BF16)
    ring_sems = pltpu.SemaphoreType.DMA((2, n_ep))
    side_sems = pltpu.SemaphoreType.DMA((2, 2, side))
    grad = jax.ShapeDtypeStruct((1, rows, hid), F32)
    shapes = (
        jax.ShapeDtypeStruct((tok, width), BF16),
        jax.ShapeDtypeStruct((1, tok), BF16),
        grad,
        grad,
        grad,
    )
    results = pl.pallas_call(
        functools.partial(kernel, cap, n_ep, side),
        out_shape=shapes,
        in_specs=[vmem] * 4 + [hbm] * 3,
        out_specs=[vmem] * 5,
        scratch_shapes=[
            weight,
            weight,
            weight,
            pltpu.VMEM((slots * blocks, LANES), F32),
            pltpu.VMEM((tok, width), BF16),
            tiled,
            tiled,
            tiled,
            tiled,
            flat,
            flat,
            narrow,
            narrow,
            tiled,
            tiled,
            probs,
            probs,
            pltpu.VMEM((2, 2, side) + slices, BF16),
            squares,
            squares,
            squares,
            pltpu.VMEM((2,) + slices, BF16),
            pltpu.VMEM((2,) + slices, BF16),
            pltpu.SemaphoreType.DMA((3,)),
            ring_sems,
            ring_sems,
            ring_sems,
            ring_sems,
            pltpu.SemaphoreType.DMA((2, 2, side * side)),
            side_sems,
            side_sems,
        ],
        compiler_params=pltpu.CompilerParams(
            collective_id=0, has_side_effects=True, vmem_limit_bytes=56 << 20
        ),
    )(
        tokens,
        cotangent,
        gate_prob.reshape(1, tok),
        expert_ids.reshape(1, tok),
        gate_weight,
        up_weight,
        down_weight,
    )
    results = pl.pallas_call(
        hand_on,
        out_shape=shapes,
        in_specs=[vmem] * 5,
        out_specs=[vmem] * 5,
    )(*results)
    return (results[0], results[1].reshape(tok, 1)) + tuple(results[2:])


def solution(mesh):
    in_specs = (
        P(("group", "ep"), None),
        P(("group", "ep"), None),
        P(("group", "ep"), None),
        P(("group", "ep"), None),
        P("ep", None, None),
        P("ep", None, None),
        P("ep", None, None),
    )
    out_specs = (
        P(("group", "ep"), None),
        P(("group", "ep"), None),
        P("ep", "group", None),
        P("ep", "group", None),
        P("ep", "group", None),
    )
    return jax.shard_map(
        per_device, mesh=mesh, in_specs=in_specs, out_specs=out_specs, check_vma=False
    )
```

time: 227 us -> 214 us (0.943)
  local copies, waits for them, and re-layouts: 10.7 us -> 0 us
    unnamed x6 -> x0, local copies, waits for them, and re-layouts: 9.35 us -> none
    pallas_call x1 -> x2, Pallas kernels: 215 us -> 213 us  [the longest x1 211 us: per_device(): pl.pallas_call(functools.partial(kernel, cap, n_ep, side), out_shape=shap...]
where the time goes in v2:
time: 214 us
  Pallas kernels  213 us (100%)
    pallas_call x1, Pallas kernels, per_device(): pl.pallas_call(functools.partial(kernel, cap, n_ep, side), out_shape=shap...  211 us

profile of v2, /device:TPU:1, one launch (start us, length us, event | category | flops | bytes accessed | tf_op | source)
XLA Modules:
  0.0 214.1 jit_solution(16534155808613146972)
XLA Ops:
  0.6 211.3 %shard_map.110 = (bf16[128,2048]{1,0:T(8,128)(2,1)}, bf16[1,128]{1,0:T(2,128)(2,1)}, f32[1,64,512]{2,1,0:T(8,128)}, f32[1,64,512]{2,1,0:T(8,128)}, f32[1,64,512]{2,1,0:T(8,128)}) custom-call(bf16[128,2048]{1,0:T(8,128)(2,1)} %x_ref.1, bf16[128,2048]{1,0:T(8,128)(2,1)} %dy_ref.1, bf16[1,128]{1,0:T(2,128)(2,1)} %bitcast.3, s32[1,128]{1,0:T(1,128)} %bitcast.4, ...), custom_call_target="tpu_custom_call" | custom-call | tf_op jit(solution)/shard_map/pallas_call | solution.py:415
  212.0 2.1 shard_map.111

commit v3 on v2

--- a/solution.py
+++ b/solution.py
@@ -84,6 +84,7 @@
     pair_sems,
     mid_sems,
     last_sems,
+    ready,
 ):
     me = lax.axis_index("ep")
     grp = lax.axis_index("group")
@@ -108,15 +109,13 @@
     def greet(device):
         pl.semaphore_signal(barrier, inc=1, device_id=device, device_id_type=MESH)
 
-    def greet_ring(k, carry):
+    for k in (1, n_ep - 1):
         greet({"ep": lax.rem(me + k, n_ep)})
-        return carry
-
-    lax.fori_loop(1, n_ep, greet_ring, 0)
     for half in range(2):
         for k in range(1, side):
             greet(on_plane(half, lax.rem(own_a[half] + k, side), own_b[half]))
     greet(sibling)
+    pl.semaphore_wait(barrier, 2 + 2 * (side - 1) + 1)
 
     weight_copies = [
         pltpu.make_async_copy(src.at[0], dst, w_sem.at[i])
@@ -124,6 +123,17 @@
     ]
     for copy in weight_copies:
         copy.start()
+
+    def tell(level):
+        for way, k in enumerate((1 << level, n_ep - (1 << level))):
+            pl.semaphore_signal(
+                ready.at[level, way],
+                inc=1,
+                device_id={"ep": lax.rem(me + k, n_ep)},
+                device_id_type=MESH,
+            )
+
+    tell(0)
 
     turned = lax.rem(ids_ref[...] + (2 * n_ep - quarter - 1) - me, n_ep).astype(F32)
     hits_t = one_hot(turned == iota((n_ep, tok), 0))
@@ -196,11 +206,24 @@
             spread(batch, placed[:, LANES:], 2 * j + 1)
         pack(batch, dst)
 
-    to_slots(0, x_ref, xs)
-    pl.semaphore_wait(barrier, n_ep - 1 + 2 * (side - 1) + 1)
+    def send_near(k):
+        out_copy(xs, xr, x_sems, k, cap).start()
+        if k < quarter:
+            out_copy(xs, xr, x_sems, n_ep - k, cap).start()
+
+    to_slots(1, x_ref, xs)
+    send_near(1)
+    levels = (n_ep // 2).bit_length() - 1
+    for level in range(levels):
+        for way in range(2):
+            pl.semaphore_wait(ready.at[level, way], 1)
+        if level < levels - 1:
+            tell(level + 1)
+            for k in range((1 << level) + 1, (2 << level) + 1):
+                send_near(k)
+        if level == 0:
+            to_slots(0, x_ref, xs)
     batch_steps(n_ep, 0, lambda k: out_copy(xs, xr, x_sems, k, cap).start())
-    to_slots(1, x_ref, xs)
-    batch_steps(n_ep, 1, lambda k: out_copy(xs, xr, x_sems, k, cap).start())
     xr[own_got * cap : (own_got + 1) * cap] = xs[own_sent * cap : (own_sent + 1) * cap]
 
     prob_row = p_ref[...].astype(F32)
@@ -255,10 +278,9 @@
         ps[batch * (n_ep // 2) : (batch + 1) * (n_ep // 2)] = prob_rows.reshape(
             n_ep // 2, 1, LANES
         )
+        batch_steps(n_ep, batch, lambda k: home_copy(ps, pr, p_sems, k, 1).start())
     yr[own_sent * cap : (own_sent + 1) * cap] = ys[own_got * cap : (own_got + 1) * cap]
     pr[own_sent : own_sent + 1] = ps[own_got : own_got + 1]
-    for batch in range(2):
-        batch_steps(n_ep, batch, lambda k: home_copy(ps, pr, p_sems, k, 1).start())
 
     contract_rows = (((0,), (0,)), ((), ()))
     few = rows // 2
@@ -449,6 +471,7 @@
             pltpu.SemaphoreType.DMA((2, 2, side * side)),
             side_sems,
             side_sems,
+            pltpu.SemaphoreType.REGULAR(((n_ep // 2).bit_length() - 1, 2)),
         ],
         compiler_params=pltpu.CompilerParams(
             collective_id=0, has_side_effects=True, vmem_limit_bytes=56 << 20

time: 214 us -> 206 us (0.963)
  Pallas kernels: 213 us -> 204 us
    pallas_call x1, Pallas kernels: 211 us -> 202 us  [per_device(): pl.pallas_call(functools.partial(kernel, cap, n_ep, side), out_shape=shap...]
where the time goes in v3:
time: 206 us; the launch traced here: 205 us
  Pallas kernels  204 us (99%)
    pallas_call x1, Pallas kernels, per_device(): pl.pallas_call(functools.partial(kernel, cap, n_ep, side), out_shape=shap...  202 us

profile of v3, /device:TPU:1, one launch (start us, length us, event | category | flops | bytes accessed | tf_op | source)
XLA Modules:
  0.0 205.1 jit_solution(14705999187292726206)
XLA Ops:
  0.6 202.4 %shard_map.110 = (bf16[128,2048]{1,0:T(8,128)(2,1)}, bf16[1,128]{1,0:T(2,128)(2,1)}, f32[1,64,512]{2,1,0:T(8,128)}, f32[1,64,512]{2,1,0:T(8,128)}, f32[1,64,512]{2,1,0:T(8,128)}) custom-call(bf16[128,2048]{1,0:T(8,128)(2,1)} %x_ref.1, bf16[128,2048]{1,0:T(8,128)(2,1)} %dy_ref.1, bf16[1,128]{1,0:T(2,128)(2,1)} %bitcast.3, s32[1,128]{1,0:T(1,128)} %bitcast.4, ...), custom_call_target="tpu_custom_call" | custom-call | tf_op jit(solution)/shard_map/pallas_call | solution.py:437
  203.0 2.1 %shard_map.111 = (bf16[128,2048]{1,0:T(8,128)(2,1)}, bf16[1,128]{1,0:T(2,128)(2,1)}, f32[1,64,512]{2,1,0:T(8,128)}, f32[1,64,512]{2,1,0:T(8,128)}, f32[1,64,512]{2,1,0:T(8,128)}) custom-call(bf16[128,2048]{1,0:T(8,128)(2,1)} %get-tuple-element.15.refs_0_, bf16[1,128]{1,0:T(2,128)(2,1)} %get-tuple-element.16.refs_1_, ...), custom_call_target="tpu_custom_call" | custom-call | tf_op jit(solution)/shard_map/pallas_call | solution.py:488

commit v4 on v3

--- a/solution.py
+++ b/solution.py
@@ -41,8 +41,8 @@
     cap,
     n_ep,
     side,
-    x_ref,
-    dy_ref,
+    x_hbm,
+    dy_hbm,
     p_ref,
     ids_ref,
     wg_hbm,
@@ -53,6 +53,8 @@
     gg_ref,
     gu_ref,
     gd_ref,
+    x_ref,
+    dy_ref,
     wg,
     wu,
     wd,
@@ -76,6 +78,7 @@
     mid_in,
     last,
     last_in,
+    row_sem,
     w_sem,
     x_sems,
     d_sems,
@@ -93,6 +96,10 @@
     n_chip = side * side
     at_y, at_x = chip // side, lax.rem(chip, side)
     tok, width = x_ref.shape
+    row_copies = [
+        pltpu.make_async_copy(x_hbm, x_ref, row_sem.at[0]),
+        pltpu.make_async_copy(dy_hbm, dy_ref, row_sem.at[1]),
+    ]
     slots = n_ep * cap
     blocks = width // LANES
     rows = width // (2 * n_chip)
@@ -115,14 +122,9 @@
         for k in range(1, side):
             greet(on_plane(half, lax.rem(own_a[half] + k, side), own_b[half]))
     greet(sibling)
+    for copy in row_copies:
+        copy.start()
     pl.semaphore_wait(barrier, 2 + 2 * (side - 1) + 1)
-
-    weight_copies = [
-        pltpu.make_async_copy(src.at[0], dst, w_sem.at[i])
-        for i, (src, dst) in enumerate(((wg_hbm, wg), (wu_hbm, wu), (wd_hbm, wd)))
-    ]
-    for copy in weight_copies:
-        copy.start()
 
     def tell(level):
         for way, k in enumerate((1 << level, n_ep - (1 << level))):
@@ -134,6 +136,12 @@
             )
 
     tell(0)
+    weight_copies = [
+        pltpu.make_async_copy(src.at[0], dst, w_sem.at[i])
+        for i, (src, dst) in enumerate(((wg_hbm, wg), (wu_hbm, wu), (wd_hbm, wd)))
+    ]
+    for copy in weight_copies:
+        copy.start()
 
     turned = lax.rem(ids_ref[...] + (2 * n_ep - quarter - 1) - me, n_ep).astype(F32)
     hits_t = one_hot(turned == iota((n_ep, tok), 0))
@@ -211,21 +219,25 @@
         if k < quarter:
             out_copy(xs, xr, x_sems, n_ep - k, cap).start()
 
-    to_slots(1, x_ref, xs)
-    send_near(1)
     levels = (n_ep // 2).bit_length() - 1
     for level in range(levels):
         for way in range(2):
             pl.semaphore_wait(ready.at[level, way], 1)
         if level < levels - 1:
             tell(level + 1)
+        if level == 0:
+            row_copies[0].wait()
+            to_slots(1, x_ref, xs)
+            send_near(1)
+        if level < levels - 1:
             for k in range((1 << level) + 1, (2 << level) + 1):
                 send_near(k)
-        if level == 0:
+        if level == max(levels - 2, 0):
             to_slots(0, x_ref, xs)
     batch_steps(n_ep, 0, lambda k: out_copy(xs, xr, x_sems, k, cap).start())
     xr[own_got * cap : (own_got + 1) * cap] = xs[own_sent * cap : (own_sent + 1) * cap]
 
+    row_copies[1].wait()
     prob_row = p_ref[...].astype(F32)
     prob = upright(prob_row)
     scaled[...] = (prob * dy_ref[...].astype(F32)).astype(BF16)
@@ -437,9 +449,11 @@
     results = pl.pallas_call(
         functools.partial(kernel, cap, n_ep, side),
         out_shape=shapes,
-        in_specs=[vmem] * 4 + [hbm] * 3,
+        in_specs=[hbm] * 2 + [vmem] * 2 + [hbm] * 3,
         out_specs=[vmem] * 5,
         scratch_shapes=[
+            pltpu.VMEM((tok, width), BF16),
+            pltpu.VMEM((tok, width), BF16),
             weight,
             weight,
             weight,
@@ -463,6 +477,7 @@
             squares,
             pltpu.VMEM((2,) + slices, BF16),
             pltpu.VMEM((2,) + slices, BF16),
+            pltpu.SemaphoreType.DMA((2,)),
             pltpu.SemaphoreType.DMA((3,)),
             ring_sems,
             ring_sems,

time: 206 us -> 206 us (level)
  no operation moved by 1% of the time
where the time goes in v4:
time: 206 us; the launch traced here: 204 us
  Pallas kernels  204 us (99%)
    pallas_call x1, Pallas kernels, per_device(): pl.pallas_call(functools.partial(kernel, cap, n_ep, side), out_shape=shap...  202 us

profile of v4, /device:TPU:1, one launch (start us, length us, event | category | flops | bytes accessed | tf_op | source)
XLA Modules:
  0.0 204.5 jit_solution(14857472361497661547)
XLA Ops:
  0.6 201.7 %shard_map.110 = (bf16[128,2048]{1,0:T(8,128)(2,1)}, bf16[1,128]{1,0:T(2,128)(2,1)}, f32[1,64,512]{2,1,0:T(8,128)}, f32[1,64,512]{2,1,0:T(8,128)}, f32[1,64,512]{2,1,0:T(8,128)}) custom-call(bf16[128,2048]{1,0:T(8,128)(2,1)} %x_hbm.1, bf16[128,2048]{1,0:T(8,128)(2,1)} %dy_hbm.1, bf16[1,128]{1,0:T(2,128)(2,1)} %bitcast.3, s32[1,128]{1,0:T(1,128)} %bitcast.4, ...), custom_call_target="tpu_custom_call" | custom-call | tf_op jit(solution)/shard_map/pallas_call | solution.py:449
  202.4 2.1 %shard_map.111 = (bf16[128,2048]{1,0:T(8,128)(2,1)}, bf16[1,128]{1,0:T(2,128)(2,1)}, f32[1,64,512]{2,1,0:T(8,128)}, f32[1,64,512]{2,1,0:T(8,128)}, f32[1,64,512]{2,1,0:T(8,128)}) custom-call(bf16[128,2048]{1,0:T(8,128)(2,1)} %get-tuple-element.15.refs_0_, bf16[1,128]{1,0:T(2,128)(2,1)} %get-tuple-element.16.refs_1_, ...), custom_call_target="tpu_custom_call" | custom-call | tf_op jit(solution)/shard_map/pallas_call | solution.py:503
